TPU v7x, 32 devices: a whole 2x2x4 slice. The times are simulated.
32 devices in a mesh: seq: 16 (over z, y, core), tp: 2 (over x).
Axes of the slice: x: 2, y: 2, z: 4, core: 2. Of those that a mesh axis runs over, the one named last changes fastest.
Arguments:
- inputs: bfloat16 [2, 2048, 2048], P(None, 'seq', 'tp'), may hold values from -6 to 6
- segments: int32 [2, 2048], P(None, 'seq'), may hold values from 0 to 12, as said below
- keys: bfloat16 [2, 2048, 2048], P(None, 'seq', 'tp'), may hold values from -9 to 9
- values: bfloat16 [2, 2048, 2048], P(None, 'seq', 'tp'), may hold values from -6 to 6
- attn_gain: float32 [2048], replicated, may hold values from 0.5 to 1.5
- query_weight: bfloat16 [2048, 2048], P(None, 'tp'), may hold values from -0.125 to 0.125
- out_weight: bfloat16 [2048, 2048], P(None, 'tp'), may hold values from -0.75 to 0.75
- ffn_gain: float32 [2048], replicated, may hold values from 0.5 to 1.5
- gate_weight: bfloat16 [2048, 5504], P(None, 'tp'), may hold values from -0.125 to 0.125
- up_weight: bfloat16 [2048, 5504], P(None, 'tp'), may hold values from -0.125 to 0.125
- down_weight: bfloat16 [2048, 5504], P(None, 'tp'), may hold values from -0.078125 to 0.078125
- cotangent: bfloat16 [2, 2048, 2048], P(None, 'seq', 'tp'), may hold values from -6 to 6
Outputs:
- mixed: bfloat16 [2, 2048, 2048], P(None, 'seq', 'tp')
- input_grad: float32 [2, 2048, 2048], P(None, 'seq', 'tp')
- key_grad: float32 [2, 2048, 2048], P(None, 'seq', 'tp')
- value_grad: float32 [2, 2048, 2048], P(None, 'seq', 'tp')
- attn_gain_grad: float32 [2048], P('seq')
- query_grad: float32 [2048, 2048], P('seq', 'tp')
- out_grad: float32 [2048, 2048], P('seq', 'tp')
- ffn_gain_grad: float32 [2048], P('seq')
- gate_grad: float32 [2048, 5504], P('seq', 'tp')
- up_grad: float32 [2048, 5504], P('seq', 'tp')
- down_grad: float32 [2048, 5504], P('seq', 'tp')
Inputs may be any that keep to these rules, and one draw needn't show every extreme that they name: `segments`: document numbers never fall along a row.
All inputs are finite; a program needn't handle non-finite values.
Results may differ from a plain program's by a relative error of at most 0.02.
Values may be sent and summed in bfloat16 or wider, within the bound.
A program may use at most 448 MiB of HBM per device.

v0:
```python
import functools
import math
import types

import jax
import jax.numpy as jnp
from jax import lax
from jax.experimental import pallas as pl
from jax.experimental.pallas import tpu as pltpu
from jax.sharding import PartitionSpec as P

HEAD_DIM = 128
CUTS = 12


EPSILON = 1e-06
NEGATIVE_FILL = -1e30

MESH = pl.DeviceIdType.MESH
BF = jnp.bfloat16
F32 = jnp.float32
VMEM_GRANT = 63 << 20
PLANE = 4
LANE = 128


def dot_nn(a, b):
    return lax.dot_general(a, b, (((1,), (0,)), ((), ())), preferred_element_type=F32)


def dot_nt(a, b):
    return lax.dot_general(a, b, (((1,), (1,)), ((), ())), preferred_element_type=F32)


def dot_tn(a, b):
    return lax.dot_general(a, b, (((0,), (0,)), ((), ())), preferred_element_type=F32)


def aligned(index, size):
    return pl.ds(pl.multiple_of(index * size, size), size)


class Place:
    def __init__(self, n):
        self.n = n
        self.s = lax.axis_index("seq")
        self.t = lax.axis_index("tp")
        self.z = self.s // PLANE
        self.p = lax.rem(self.s, PLANE)
        self.y = self.p // 2
        self.c = lax.rem(self.p, 2)
        base = self.z * PLANE
        self.core_p = self.y * 2 + 1 - self.c
        self.side_p = (1 - self.y) * 2 + self.c
        self.cross_p = (1 - self.y) * 2 + 1 - self.c
        self.core = (base + self.core_p, self.t)
        self.side = (base + self.side_p, self.t)
        self.cross = (base + self.cross_p, self.t)
        self.twin = (self.s, 1 - self.t)

    def other(self, k):
        return lax.rem(self.s + k, self.n)

    def enter(self):
        barrier = pltpu.get_barrier_semaphore()

        def greet(k, unused):
            pl.semaphore_signal(barrier, inc=1, device_id=(self.other(k), self.t), device_id_type=MESH)
            return unused

        lax.fori_loop(1, self.n, greet, 0)
        pl.semaphore_signal(barrier, inc=1, device_id=self.twin, device_id_type=MESH)
        pl.semaphore_wait(barrier, self.n)


def remote(src, dst, send, recv, device):
    return pltpu.make_async_remote_copy(
        src_ref=src, dst_ref=dst, send_sem=send, recv_sem=recv, device_id=device, device_id_type=MESH
    )


class Spread:
    def __init__(self, place, src, dst, send, recv, local, bulk):
        self.place, self.src, self.dst, self.send, self.recv, self.local = place, src, dst, send, recv, local
        self.bulk = bulk

    def copy(self, k):
        place = self.place
        d = place.other(k)
        return remote(self.src(d), self.dst(), self.send, self.recv, (d, place.t))

    def own(self):
        return pltpu.make_async_copy(self.src(self.place.s), self.dst(), self.local)

    def start(self):
        self.own().start()

        def one(k, unused):
            self.copy(k).start()
            return unused

        lax.fori_loop(1, self.place.n, one, 0)

    def start_to(self, d, unused):
        k = lax.rem(d - self.place.s + self.place.n, self.place.n)

        @pl.when(k == 0)
        def _():
            self.own().start()

        @pl.when(k != 0)
        def _():
            self.copy(k).start()

        return unused

    def wait(self):
        self.own().wait()
        remote(self.bulk, self.bulk, self.send, self.recv, self.place.core).wait()


def attention_masks(seg_all, seg_row, seg_col, n, tok):
    def one(i, unused):
        piece = seg_all[i].astype(F32)
        seg_row[:, aligned(i, tok)] = piece
        seg_col[aligned(i, tok), :] = jnp.transpose(jnp.broadcast_to(piece, (tok, tok)))
        return unused

    lax.fori_loop(0, n, one, 0)


def readable(seg_col, seg_row, key_block, query_block, block):
    key_seg = seg_col[aligned(key_block, block), :]
    key_seg = jnp.concatenate([key_seg] * (block // LANE), axis=1)
    query_seg = seg_row[:, aligned(query_block, block)]
    key_pos = key_block * block + lax.broadcasted_iota(jnp.int32, (block, block), 0)
    query_pos = query_block * block + lax.broadcasted_iota(jnp.int32, (block, block), 1)
    return (key_seg == query_seg) & (key_pos <= query_pos)


def split_rows(whole, split, n):
    blk = whole.shape[1] * 2 // n
    for zy in range(n // 2):
        z, y = divmod(zy, 2)
        split[y, :, z * blk : (z + 1) * blk] = whole[:, zy * blk : (zy + 1) * blk]


class Plane:
    def __init__(self, place, split, left, send, recv, local, tokens):
        self.place, self.tokens, self.left = place, tokens, left
        to = left.at[aligned(place.p, tokens), :]
        self.own = pltpu.make_async_copy(split.at[place.y], to, local)
        self.to_core = remote(split.at[place.y], to, send.at[0], recv.at[0], place.core)
        self.to_side = remote(split.at[1 - place.y], to, send.at[1], recv.at[1], place.side)
        passed = left.at[aligned(place.side_p, tokens), :]
        self.on = remote(passed, passed, send.at[2], recv.at[2], place.core)

    def start(self):
        self.to_side.start()
        self.own.start()
        self.to_core.start()

    def forward(self):
        self.to_side.wait()
        self.on.start()

    def gone(self):
        self.own.wait()
        self.to_core.wait_send()

    def finish(self):
        self.to_core.wait_recv()
        self.on.wait()


def vm(shape, dtype):
    return jax.ShapeDtypeStruct(shape, dtype)


class Gather:
    def __init__(self, place, whole, stride, first, land, send, recv, local, tokens):
        cols = land.shape[1]
        to = land.at[aligned(place.p, tokens), :]

        def half(c):
            return whole.at[:, pl.ds(pl.multiple_of(c * stride + first, LANE), cols)]

        c = place.c
        self.own = pltpu.make_async_copy(half(c), to, local)
        self.away = [
            remote(half(c), to, send.at[0], recv.at[0], place.side),
            remote(half(1 - c), to, send.at[1], recv.at[1], place.cross),
            remote(half(1 - c), to, send.at[2], recv.at[2], place.core),
        ]

    def start(self):
        self.own.start()
        for copy in self.away:
            copy.start()

    def wait(self):
        self.own.wait()
        for copy in self.away:
            copy.wait()


class Line:
    def __init__(self, place, nz, blk, gather, land, left, lv, mv, move, got, total, out, turned, sems, work):
        self.place, self.nz, self.blk, self.gather = place, nz, blk, gather
        self.land, self.left, self.move, self.got, self.total, self.out = land, left, move, got, total, out
        self.turned = turned
        self.cols = land.shape[1]
        self.lv, self.mv = lv, mv
        self.acc, self.stage, self.load_sem = work
        self.send, self.recv, self.end_s, self.end_r, self.end_l = sems
        self.at_end = (place.z == 0) | (place.z == nz - 1)

    def load(self, left_too=False, gathered=False):
        if not gathered:
            self.gather.wait()
        copies = []
        if self.land is not self.mv:
            copies.append(pltpu.make_async_copy(self.land, self.mv, self.load_sem.at[0]))
        if left_too and self.left is not self.lv:
            copies.append(pltpu.make_async_copy(self.left, self.lv, self.load_sem.at[1]))
        for copy in copies:
            copy.start()
        for copy in copies:
            copy.wait()

    def product(self, b):
        tile = 2 * LANE

        def one(i, unused):
            at = pl.ds(pl.multiple_of(jnp.minimum(i * tile, self.cols - tile), LANE), tile)
            self.acc[:, at] = dot_tn(self.lv[:, aligned(b, self.blk)], self.mv[:, at])
            return unused

        lax.fori_loop(0, -(-self.cols // tile), one, 0)

    def take(self, slot):
        self.arrival(slot).wait_recv()
        copy = pltpu.make_async_copy(self.got.at[slot], self.stage.at[:, : self.cols], self.load_sem.at[2])
        copy.start()
        copy.wait()
        return self.stage[:, : self.cols].astype(F32)

    def arrival(self, slot):
        return remote(self.move.at[0], self.got.at[slot], self.send.at[0], self.recv.at[slot], self.place.core)

    def route(self, j):
        z, nz = self.place.z, self.nz
        b = jnp.where(z < nz // 2, nz - 1 - j, j)
        b = jnp.where((j == nz - 2) & (z == 1), 0, b)
        b = jnp.where((j == nz - 2) & (z == nz - 2), nz - 1, b)
        b = jnp.where(j == nz - 1, z, b)
        up = b > z
        to = jnp.where(up, z + 1, z - 1)
        slot_in = jnp.where(up, b - z, nz - z + b)
        slot_out = jnp.where(up, b - to, nz - to + b)
        keep = jnp.where(up, b - 1, b)
        last = jnp.where(up, z == 0, z == nz - 1)
        device = (to * PLANE + self.place.p, self.place.t)

        def out():
            return remote(self.move.at[keep], self.got.at[slot_out], self.send.at[keep], self.recv.at[slot_out], device)

        return b, slot_in, keep, last, out

    def step(self, j):
        b, slot_in, keep, last, out = self.route(j)
        self.product(b)
        sends = j < self.nz - 1

        @pl.when(jnp.logical_not(sends))
        def _():
            self.total[...] = self.acc[:, : self.cols]

        @pl.when(sends & last)
        def _():
            self.move[keep] = self.acc[:, : self.cols].astype(BF)

        @pl.when(sends & jnp.logical_not(last))
        def _():
            self.move[keep] = (self.acc[:, : self.cols] + self.take(slot_in)).astype(BF)

        @pl.when(sends)
        def _():
            out().start()

    def steps(self, low, high):
        def one(j, unused):
            self.step(j)
            return unused

        lax.fori_loop(low, high, one, 0)

    def some(self, *order):
        def one(i, unused):
            j = order[0]
            for k, then in enumerate(order):
                j = jnp.where(i == k, then, j)
            self.step(j)
            return unused

        lax.fori_loop(0, len(order), one, 0)

    def begin(self):
        self.steps(0, self.nz)

    def from_end(self):
        self.steps(jnp.where(self.at_end, 0, self.nz - 1), self.nz)

    def between(self, low, high):
        pl.when(jnp.logical_not(self.at_end))(lambda: self.steps(low, high))

    def sent(self):
        def one(j, unused):
            self.route(j)[4]().wait_send()
            return unused

        lax.fori_loop(0, self.nz - 1, one, 0)

    def end(self, c):
        half = self.blk // 2
        mine = self.place.c
        if self.turned is None:
            return self.out.at[:, aligned(mine, self.cols)], self.total.at[aligned(c, half), :]
        turned, stride, first = self.turned
        to = self.out.at[pl.ds(pl.multiple_of(mine * stride + first, LANE), self.cols), :]
        return to, turned.at[first : first + self.cols, aligned(c, half)]

    def away(self):
        to, theirs = self.end(1 - self.place.c)
        return remote(theirs, to, self.end_s, self.end_r, self.place.core)

    def here(self):
        to, mine = self.end(self.place.c)
        return pltpu.make_async_copy(mine, to, self.end_l)

    def finish(self):
        z, nz = self.place.z, self.nz

        @pl.when(z > 0)
        def _():
            self.total[...] += self.take(0)

        @pl.when(z < nz - 1)
        def _():
            self.total[...] += self.take(nz)

        if self.turned is not None:
            turned, _, first = self.turned
            turned[first : first + self.cols, :] = jnp.transpose(self.total[...])
        self.away().start()
        self.here().start()

    def left_here(self):
        self.away().wait_send()
        self.here().wait()

    def arrived(self):
        self.away().wait_recv()


class Weights:
    def __init__(self, weights, buffers, sems, tail_sems, phase, first, cols, ff):
        self.weights, self.buffers, self.sems, self.tail_sems, self.phase = weights, buffers, sems, tail_sems, phase
        self.first, self.each = first, len(weights)
        self.size = buffers.shape[1]
        self.cols = cols
        self.regular = 2 * (cols // self.size)
        self.rest = cols % self.size
        self.rest_two = ff - cols - cols // self.size * self.size

    def slot(self, i, w):
        return self.first + lax.rem(i + self.phase, 2) * self.each + w

    def copies(self, i):
        at = pl.ds(pl.multiple_of(lax.rem(i, 2) * self.cols + i // 2 * self.size, LANE), self.size)
        return [
            pltpu.make_async_copy(ref.at[at, :], self.buffers.at[self.slot(i, w)], self.sems.at[lax.rem(i, 2), w])
            for w, ref in enumerate(self.weights)
        ]

    def tail(self):
        first = self.cols // self.size * self.size
        copies = []
        for w, ref in enumerate(self.weights):
            to = self.buffers.at[self.slot(self.regular, w)]
            copies += [
                pltpu.make_async_copy(ref.at[pl.ds(first, self.rest), :], to.at[pl.ds(0, self.rest), :], self.tail_sems.at[0, w]),
                pltpu.make_async_copy(
                    ref.at[pl.ds(self.cols + first, self.rest_two), :],
                    to.at[pl.ds(self.rest, self.rest_two), :],
                    self.tail_sems.at[1, w],
                ),
            ]
        return copies

    def begin(self, blocks=1):
        self.begun = blocks
        for i in range(blocks):
            for copy in self.copies(i):
                copy.start()

    def run(self, work, after=()):
        first = self.cols // self.size * self.size
        filled = self.rest + self.rest_two

        def one(i, unused):
            is_tail = i == self.regular

            @pl.when((i + 1 < self.regular) & (i + 1 >= self.begun))
            def _():
                for copy in self.copies(i + 1):
                    copy.start()

            @pl.when(i + 1 == self.regular)
            def _():
                for copy in self.tail():
                    copy.start()

            @pl.when(jnp.logical_not(is_tail))
            def _():
                for copy in self.copies(i):
                    copy.wait()

            @pl.when(is_tail)
            def _():
                for copy in self.tail():
                    copy.wait()
                for w in range(self.each):
                    slot = self.slot(self.regular, w)
                    self.buffers[slot, filled:, :] = jnp.zeros((self.size - filled, self.buffers.shape[2]), BF)

            at = lax.rem(i, 2) * self.cols + i // 2 * self.size
            columns = [
                pl.ds(pl.multiple_of(jnp.where(is_tail, tail_at, at + k * LANE), LANE), LANE)
                for k, tail_at in enumerate((first, self.cols + first))
            ]
            work([self.slot(i, w) for w in range(self.each)], columns)
            for at_block, things in after:
                pl.when(i == at_block)(lambda things=things: [thing() for thing in things] and None)
            return unused

        lax.fori_loop(0, self.regular + 1, one, 0)


class Units:
    def __init__(self, place, nz, heads, tok):
        self.place, self.nz, self.heads, self.tok = place, nz, heads, tok
        z, s = place.z, place.s
        self.at_end = (z == 0) | (z == nz - 1)
        self.second = jnp.where(z < nz // 2, s - PLANE, s + PLANE)
        self.near = (jnp.where(z == 0, s + PLANE, s - PLANE), place.t)

    def host(self, u):
        z = u // PLANE
        inner = jnp.clip(z, 1, self.nz - 2)
        return inner * PLANE + lax.rem(u, PLANE), jnp.where(inner == z, 0, 1)

    def unit(self, slot):
        return jnp.where(slot == 0, self.place.s, self.second)

    def home(self, ref, u):
        return ref.at[aligned(u // self.heads, self.tok), aligned(lax.rem(u, self.heads), HEAD_DIM)]


class ToUnits:
    def __init__(self, units, src, land, send, recv, local):
        self.units, self.src, self.land, self.send, self.recv, self.local = units, src, land, send, recv, local
        self.n, self.s, self.t, self.tok = units.place.n, units.place.s, units.place.t, units.tok

    def away(self, u):
        host, slot = self.units.host(u)
        to = self.land.at[slot, aligned(self.s, self.tok), :]
        return remote(self.units.home(self.src, u), to, self.send, self.recv.at[slot], (host, self.t))

    def here(self, u):
        slot = self.units.host(u)[1]
        to = self.land.at[slot, aligned(self.s, self.tok), :]
        return pltpu.make_async_copy(self.units.home(self.src, u), to, self.local.at[slot])

    def start(self, u, unused):
        host = self.units.host(u)[0]
        pl.when(host == self.s)(lambda: self.here(u).start())
        pl.when(host != self.s)(lambda: self.away(u).start())
        return unused

    def bulk(self, copies, recv):
        some = self.land.at[0, pl.ds(0, copies * self.tok), :]
        return remote(some, some, self.send, recv, self.units.place.core)

    def wait(self, slot):
        self.here(self.units.unit(slot)).wait()
        self.bulk(self.n - 1, self.recv.at[slot]).wait_recv()

    def sent(self):
        pl.when(self.units.at_end)(lambda: self.bulk(self.n, self.recv.at[0]).wait_send())
        pl.when(jnp.logical_not(self.units.at_end))(lambda: self.bulk(self.n - 2, self.recv.at[0]).wait_send())


class FromUnits:
    def __init__(self, units, src, whole, send, recv, local):
        self.units, self.src, self.whole, self.send, self.recv, self.local = units, src, whole, send, recv, local
        self.n, self.s, self.t, self.tok = units.place.n, units.place.s, units.place.t, units.tok

    def away(self, slot, d):
        u = self.units.unit(slot)
        src = self.src.at[slot, aligned(d, self.tok), :]
        return remote(src, self.units.home(self.whole, u), self.send.at[slot], self.recv, (d, self.t))

    def here(self, slot):
        src = self.src.at[slot, aligned(self.s, self.tok), :]
        return pltpu.make_async_copy(src, self.units.home(self.whole, self.units.unit(slot)), self.local.at[slot])

    def start(self, slot, low, high):
        def one(d, unused):
            pl.when(d == self.s)(lambda: self.here(slot).start())
            pl.when(d != self.s)(lambda: self.away(slot, d).start())
            return unused

        lax.fori_loop(low, high, one, 0)

    def bulk(self, copies, slot):
        some = self.src.at[0, pl.ds(0, copies * self.tok), :]
        return remote(some, some, self.send.at[slot], self.recv, self.units.place.core)

    def wait(self):
        pl.when(self.units.at_end)(lambda: self.bulk(self.n, 0).wait_recv())

        @pl.when(jnp.logical_not(self.units.at_end))
        def _():
            for slot in range(2):
                self.here(slot).wait()
            self.bulk(self.n - 2, 0).wait_recv()

    def sent(self, slot):
        self.bulk(self.n - 1, slot).wait_send()


def layer_kernel(
    geo, sizes, names,
    x_in, cot_in, key_in, value_in, seg_in, wg_in, wu_in, wd_in, wo_in, wq_in, gain_one, gain_two, *refs,
):
    n, rows, tok, width, half, heads, length = geo
    ff, cols, cuts = sizes
    r = types.SimpleNamespace(**dict(zip(names, refs, strict=True)))
    tokens = rows * tok
    blk = 2 * width // n
    nz = n // PLANE
    place = Place(n)
    s, t, z = place.s, place.t, place.z
    row_s, head_s = s // heads, lax.rem(s, heads)
    mine = aligned(t, half)
    chunk = tokens // 4
    fine = 32
    wbuf = r.wbuf
    size = wbuf.shape[1]
    mid, x_all, cot_all, two_norm, two_own, two_in, one_in = (
        r.mid, r.x_all, r.cot_all, r.two_norm, r.two_own, r.two_in, r.one_in
    )
    mixed, err, one, attended, dq = r.mixed, r.err, r.one, r.attended, r.dq
    d_att = attended
    hidden, d_gate, d_up, sums = r.hidden, r.d_gate, r.d_up, r.sums
    uq, uk, uv, uo, lse, k_t = (ref.at[0] for ref in (r.uqs, r.uks, r.uvs, r.uos, r.lses, r.k_ts))
    delta = r.delta
    seg_all, seg_row, seg_col = r.seg_all, r.seg_row, r.seg_col
    udq, udk, udv = r.udq, r.udk, r.udv
    tp_s, tp_r, a_s, a_r, loc = r.tp_s, r.tp_r, r.a_s, r.a_r, r.loc
    units = Units(place, nz, heads, tok)
    at_end = units.at_end
    place.enter()

    to_x = remote(x_in, x_all.at[:, mine], tp_s.at[0], tp_r.at[0], place.twin)
    to_x.start()
    own_x = pltpu.make_async_copy(x_in, x_all.at[:, mine], loc.at[0])
    own_x.start()

    def piece(ref):
        return lambda d: ref.at[aligned(d // heads, tok), aligned(lax.rem(d, heads), HEAD_DIM)]

    keys = Spread(place, piece(key_in), lambda: uk.at[aligned(s, tok), :], a_s.at[0], a_r.at[0], loc.at[2], uk.at[: length - tok, :])
    vals = Spread(place, piece(value_in), lambda: uv.at[aligned(s, tok), :], a_s.at[1], a_r.at[1], loc.at[3], uv.at[: length - tok, :])
    segs = Spread(place, lambda d: seg_in.at[d // heads], lambda: seg_all.at[s], a_s.at[2], a_r.at[2], loc.at[4], seg_all.at[: n - 1])
    qrys = Spread(place, piece(dq), lambda: uq.at[aligned(s, tok), :], a_s.at[3], a_r.at[3], loc.at[5], uq.at[: length - tok, :])
    segs.start()
    keys.start()
    vals.start()
    to_cot = remote(cot_in, cot_all.at[:, mine], tp_s.at[1], tp_r.at[1], place.twin)
    to_cot.start()
    own_cot = pltpu.make_async_copy(cot_in, cot_all.at[:, mine], loc.at[6])
    own_cot.start()

    def square_copies(k, ref, sems):
        copies = []
        for zy in range(n // 2):
            to = wbuf.at[4 * k + zy // 2, :, (zy % 2) * half : (zy % 2 + 1) * half]
            copies.append(pltpu.make_async_copy(ref.at[zy * blk : (zy + 1) * blk, :], to, sems.at[zy]))
        return copies

    def square_block(k, zy):
        return wbuf[4 * k + zy // 2, :, (zy % 2) * half : (zy % 2 + 1) * half]

    def split_block(ref, at, zy):
        zz, yy = divmod(zy, 2)
        return ref[yy, at, zz * blk : (zz + 1) * blk]

    def store_split(ref, at, now):
        for zy in range(n // 2):
            zz, yy = divmod(zy, 2)
            ref[yy, at, zz * blk : (zz + 1) * blk] = now[:, zy * blk : (zy + 1) * blk]

    load_wq = square_copies(1, wq_in, r.o_sem.at[0])
    load_wo = square_copies(0, wo_in, r.o_sem.at[1])
    for copy in load_wq + load_wo:
        copy.start()
    own_x.wait()
    to_x.wait()

    def first_norm(i, unused):
        at = aligned(i, fine)
        x = x_all[at, :].astype(F32)
        root = lax.rsqrt(jnp.mean(x * x, axis=-1, keepdims=True) + EPSILON)
        store_split(one, at, (x * root * gain_one[...]).astype(BF))
        return unused

    lax.fori_loop(0, tokens // fine, first_norm, 0)
    for copy in load_wq:
        copy.wait()
    every = slice(0, tokens)
    total = jnp.zeros((tokens, half), F32)
    for zy in range(n // 2):
        total += dot_nn(split_block(one, every, zy), square_block(1, zy))
    dq[...] = (total * HEAD_DIM ** (-0.5)).astype(BF)
    qrys.start()
    lv_one, lv_two = r.lv_one, r.lv_two
    left_cot, left_two, left_err, left_one = (
        Plane(place, split, land, r.le_s.at[i], r.le_r.at[i], r.l_loc.at[i], tokens)
        for i, (split, land) in enumerate(((err, lv_one), (mixed, lv_two), (err, r.l_err), (one, r.l_one)))
    )
    left_one.start()

    segs.wait()
    attention_masks(seg_all, seg_row, seg_col, n, tok)
    keys.wait()
    vals.wait()

    def turn_into(ref, to):
        def turn(i, unused):
            at = aligned(i, tok)
            to[:, at] = jnp.transpose(ref[at, :].astype(F32)).astype(BF)
            return unused

        lax.fori_loop(0, n, turn, 0)

    turn_into(uv, k_t)
    qrys.wait()
    block = 512
    owners = block // tok
    back = Spread(
        place,
        lambda d: uo.at[aligned(d, tok), :],
        lambda: attended.at[aligned(row_s, tok), aligned(head_s, HEAD_DIM)],
        a_s.at[4], a_r.at[4], loc.at[8], uo.at[: length - tok, :],
    )

    def query_step(qi, unused):
        query_block = uq[aligned(qi, block), :]

        def key_step(j, carry):
            top, total, acc = carry
            kj = qi - j
            scores = dot_nt(uk[aligned(kj, block), :], query_block)
            scores = jnp.where(readable(seg_col, seg_row, kj, qi, block), scores, NEGATIVE_FILL)
            new_top = jnp.maximum(top, jnp.max(scores, axis=0, keepdims=True))
            weights = jnp.exp(scores - new_top)
            decay = jnp.exp(top - new_top)
            total = total * decay + jnp.sum(weights, axis=0, keepdims=True)
            acc = acc * decay + dot_nn(k_t[:, aligned(kj, block)], weights.astype(BF))
            return new_top, total, acc

        start = (
            jnp.full((1, block), NEGATIVE_FILL, F32),
            jnp.zeros((1, block), F32),
            jnp.zeros((HEAD_DIM, block), F32),
        )
        top, total, acc = lax.fori_loop(0, qi + 1, key_step, start)
        lse[:, aligned(qi, block)] = top + jnp.log(total)
        uo[aligned(qi, block), :] = jnp.transpose(acc / total).astype(BF)
        return lax.fori_loop(qi * owners, (qi + 1) * owners, back.start_to, unused)

    lax.fori_loop(0, length // block, query_step, 0)

    work = (r.acc, r.stage, r.work_sem)
    mv, turned = r.mv, r.turned
    s_first, s_second, t_first, t_second = r.s_first, r.s_second, r.t_first, r.t_second
    sources = (hidden, d_gate, d_up)
    lefts_of = ((lv_one, lv_one), (lv_two, lv_two), (lv_two, lv_two))
    kept = ((s_first, t_first, r.out_down), (s_second, t_second, r.out_gate), (s_first, t_first, r.out_up))
    gots = (r.g0, r.g1, r.g2, r.g3, r.g4, r.g5, r.g6)
    lands = (None, None, None, r.m3, r.m4, r.m5, r.m6)
    plans = []
    for i, (kind, first, wide) in enumerate(cuts):
        at = pl.ds(first, wide)
        left, lv = lefts_of[kind]
        move, total_ref, out_ref = kept[kind]
        here = mv.at[:, at]
        plans.append((
            (sources[kind], cols, first), here if lands[i] is None else lands[i], left, lv, here, move.at[:, :, at], gots[i], total_ref.at[:, at],
            out_ref, (turned, cols, first),
        ))
    for source, left, lv, *rest in (
        (attended, r.l_err, lv_one, r.mv_out, r.s_out, r.g_out, r.t_out, r.out_out),
        (dq, r.l_one, lv_two, r.mv_query, r.s_query, r.g_query, r.t_query, r.out_query),
    ):
        plans.append(((source, half // 2, 0), rest[0], left, lv, *rest, None))
    lines = []
    for i, (source, land, *rest) in enumerate(plans):
        gather = Gather(place, *source, land, r.me_s.at[i], r.me_r.at[i], r.g_loc.at[i], tokens)
        sems = (r.c_s.at[i], r.c_r.at[i], r.e_s.at[i], r.e_r.at[i], r.e_l.at[i])
        lines.append(Line(place, nz, blk, gather, land, *rest, sems, work))
    down_a, down_b, down_c, gate_a, gate_b, up_a, up_b, out, query = lines
    ship = [
        remote(a.at[0], a.at[1], r.sh_s.at[i], r.sh_r.at[i], units.near)
        for i, a in enumerate((r.uqs, r.uks, r.uvs, r.uos, r.lses))
    ]

    @pl.when(at_end)
    def _():
        for copy in ship:
            copy.start()

    own_cot.wait()
    to_cot.wait()

    def split_cot(i, unused):
        at = aligned(i, fine)
        store_split(err, at, cot_all[at, :])
        return unused

    lax.fori_loop(0, tokens // fine, split_cot, 0)
    left_cot.start()
    left_one.forward()
    for copy in load_wo:
        copy.wait()
    back.wait()

    chunks = 4
    wide = width // chunks

    def to_twin(i):
        at = slice(i * wide, (i + 1) * wide)
        return remote(two_own.at[:, at], one_in.at[:, at], tp_s.at[9 + i], tp_r.at[9 + i], place.twin)

    for i in range(chunks):
        for zy in range(2 * i, 2 * i + 2):
            two_own[:, zy * blk : (zy + 1) * blk] = dot_nt(attended[...], square_block(0, zy)).astype(BF)
        to_twin(i).start()
    out.gather.start()
    zeroth_pass = Weights((wd_in,), wbuf, r.w_sem.at[3], r.tail_sem.at[3], 0, 4, cols, ff)
    first_pass = Weights((wg_in, wu_in), wbuf, r.w_sem.at[0], r.tail_sem.at[0], 0, 0, cols, ff)
    second_pass = Weights((wg_in, wu_in), wbuf, r.w_sem.at[1], r.tail_sem.at[1], 0, 4, cols, ff)
    third_pass = Weights((wd_in,), wbuf, r.w_sem.at[2], r.tail_sem.at[2], 0, 4, cols, ff)
    zeroth_pass.begin(2)
    first_pass.begin(2)

    def to_hidden(slots, at):
        now = dot_nt(cot_all[...], wbuf[slots[0]]).astype(BF)
        for k in range(2):
            d_gate[:, at[k]] = now[:, k * LANE : (k + 1) * LANE]

    zeroth_pass.run(to_hidden)
    left_cot.forward()
    square = jnp.zeros((tokens, 1), F32)
    for i in range(chunks):
        to_twin(i).wait()
        at = slice(i * wide, (i + 1) * wide)
        now = x_all[:, at].astype(F32) + (two_own[:, at].astype(F32) + one_in[:, at].astype(F32))
        mid[:, at] = now
        square += jnp.sum(now * now, axis=-1, keepdims=True)
    root_two = lax.rsqrt(square * (1.0 / width) + EPSILON)
    for i in range(chunks):
        at = slice(i * wide, (i + 1) * wide)
        two_norm[:, at] = (mid[:, at] * root_two * gain_two[:, at]).astype(BF)

    def units_block(slots, at):
        x = two_norm[...]
        gate_now, up_now = (dot_nt(x, wbuf[slot]) for slot in slots)
        d_hid = jnp.concatenate([d_gate[:, at[0]], d_gate[:, at[1]]], axis=1).astype(F32)
        sigma = jax.nn.sigmoid(gate_now)
        act = gate_now * sigma
        for ref, now in (
            (hidden, act * up_now),
            (d_gate, d_hid * up_now * sigma * (1.0 + gate_now * (1.0 - sigma))),
            (d_up, d_hid * act),
        ):
            now = now.astype(BF)
            for k in range(2):
                ref[:, at[k]] = now[:, k * LANE : (k + 1) * LANE]

    done_a, done_b = (2 * ((first + wide) // size) for _, first, wide in cuts[:2])

    def split_two(i, unused):
        at = aligned(i, fine)
        store_split(mixed, at, two_norm[at, :])
        return unused

    def begin_down():
        down_a.gather.start()
        lax.fori_loop(0, tokens // fine, split_two, 0)

    def go_on_down():
        down_b.gather.start()
        left_cot.gone()
        left_cot.finish()
        down_a.load()
        down_a.from_end()

    first_pass.run(
        units_block,
        ((done_a - 1, [begin_down]), (done_b - 1, [go_on_down]), (first_pass.regular - 1, [second_pass.begin])),
    )
    down_c.gather.start()
    left_two.start()
    down_b.load()
    down_b.from_end()
    down_a.between(0, 2)

    def block_of(ref, at):
        return jnp.concatenate([ref[:, at[0]], ref[:, at[1]]], axis=1)

    def add_up(pairs):
        for db in range(width // size):
            at = slice(db * size, (db + 1) * size)
            sums[db * tokens : (db + 1) * tokens, :] += sum(dot_nn(a, wbuf[slot, :, at]) for a, slot in pairs)

    def back_units(slots, at):
        add_up([(block_of(d_gate, at), slots[0]), (block_of(d_up, at), slots[1])])

    sums[...] = jnp.zeros_like(sums)
    second_pass.run(back_units)
    for db in range(width // size):
        two_own[:, db * size : (db + 1) * size] = sums[db * tokens : (db + 1) * tokens, :].astype(BF)

    def two_copy(i):
        at = aligned(i, chunk)
        return remote(two_own.at[at, :], two_in.at[at, :], tp_s.at[2 + i], tp_r.at[2 + i], place.twin)

    for i in range(4):
        two_copy(i).start()
    load_wo = square_copies(0, wo_in, r.o_sem.at[2])
    for copy in load_wo:
        copy.start()
    gate_a.gather.start()
    down_a.between(2, 3)
    down_b.between(0, 2)
    down_c.load()
    down_c.from_end()

    third_pass.begin()
    sums[...] = jnp.zeros_like(sums)

    def out_units(slots, at):
        add_up([(block_of(hidden, at), slots[0])])

    third_pass.run(out_units)
    left_two.forward()
    left_two.gone()
    for db in range(width // size):
        per = half // size
        mixed[db // per, :, (db % per) * size : (db % per + 1) * size] = sums[db * tokens : (db + 1) * tokens, :].astype(BF)
    ffn_copy = remote(mixed.at[1 - t], r.ffn_in, tp_s.at[6], tp_r.at[6], place.twin)
    ffn_copy.start()
    per = half // size
    for i in range(per):
        at = t * per + i
        sums[aligned(at, tokens), :] += mid[:, aligned(at, size)]
    hold = pltpu.make_async_copy(sums.at[aligned(t, per * tokens), :], r.mix, loc.at[11])
    hold.start()
    load_wq = square_copies(1, wq_in, r.o_sem.at[3])
    for copy in load_wq:
        copy.start()
    down_b.between(2, 3)
    down_c.between(0, 2)
    hold.wait()

    to_units = ToUnits(units, d_att, r.udo, r.u_s.at[0], r.u_r, r.u_l)
    out.gather.wait()
    for copy in load_wo:
        copy.wait()

    def second_norm(i, gain_sum):
        two_copy(i).wait()

        def some(j, gain_sum):
            at = aligned(i * (chunk // fine) + j, fine)
            m = mid[at, :]
            d2 = two_own[at, :].astype(F32) + two_in[at, :].astype(F32)
            root = lax.rsqrt(jnp.mean(m * m, axis=-1, keepdims=True) + EPSILON)
            gained = d2 * gain_two[...]
            scaled = m * root
            gain_sum = gain_sum + jnp.sum(d2 * scaled, axis=0, keepdims=True)
            slope = jnp.mean(gained * scaled, axis=-1, keepdims=True)
            dm = cot_all[at, :].astype(F32) + root * (gained - scaled * slope)
            mid[at, :] = dm
            store_split(err, at, dm.astype(BF))
            return gain_sum

        gain_sum = lax.fori_loop(0, chunk // fine, some, gain_sum)
        at = aligned(i, chunk)
        total = jnp.zeros((chunk, half), F32)
        for zy in range(n // 2):
            total += dot_nn(split_block(err, at, zy), square_block(0, zy))
        d_att[at, :] = total.astype(BF)
        return gain_sum

    gain_sum = jnp.zeros((1, width), F32)
    per_row = tok // chunk
    for row in range(rows):
        gain_sum = lax.fori_loop(row * per_row, (row + 1) * per_row, second_norm, gain_sum)
        lax.fori_loop(row * heads, (row + 1) * heads, to_units.start, 0)
    gain_part, gain_in = r.gain_part, r.gain_in
    for i in range(n):
        gain_part[0, i] = gain_sum[:, i * (width // n) : (i + 1) * (width // n)]
    spread_gain = [
        Spread(place, lambda d, g=g: gain_part.at[g, d], lambda g=g: gain_in.at[g, s], a_s.at[5 + g], a_r.at[5 + g], loc.at[9 + g],
               gain_in.at[g, : n - 1])
        for g in range(2)
    ]
    spread_gain[0].start()
    gate_b.gather.start()
    down_c.between(2, 3)
    left_two.finish()
    gate_a.load()
    gate_a.from_end()

    back_dq, back_dk, back_dv = (
        FromUnits(units, src, whole, r.f_s.at[i], r.f_r.at[i], r.f_l.at[i])
        for i, (src, whole) in enumerate(((udq, dq), (udk, r.d_keys), (udv, r.d_values)))
    )

    def one_unit(slot, unused):
        unit_q, unit_k, unit_v, unit_o, unit_lse, unit_kt = (
            ref.at[slot] for ref in (r.uqs, r.uks, r.uvs, r.uos, r.lses, r.k_ts)
        )
        unit_do = r.udo.at[slot]
        sums[...] = jnp.zeros_like(sums)
        to_units.wait(slot)

        def turn_delta(i, unused):
            at = aligned(i, tok)
            both = unit_do[at, :].astype(F32) * unit_o[at, :].astype(F32)
            delta[:, at] = jnp.sum(jnp.transpose(both), axis=0, keepdims=True)
            return unused

        lax.fori_loop(0, n, turn_delta, 0)

        def query_step(i, unused_too):
            qi = length // block - 1 - i
            qat = aligned(qi, block)
            qb, dob = unit_q[qat, :], unit_do[qat, :]

            def key_step(kj, dq_t):
                kat = aligned(kj, block)
                scores = dot_nt(unit_k[kat, :], qb) - unit_lse[:, qat]
                probs = jnp.exp(jnp.where(readable(seg_col, seg_row, kj, qi, block), scores, NEGATIVE_FILL))
                d_probs = dot_nt(unit_v[kat, :], dob)
                d_scores = (probs * (d_probs - delta[:, qat])).astype(BF)
                sums[kat, :HEAD_DIM] += dot_nn(d_scores, qb)
                sums[kat, HEAD_DIM:] += dot_nn(probs.astype(BF), dob)
                return dq_t + dot_nn(unit_kt[:, kat], d_scores)

            dq_t = lax.fori_loop(0, qi + 1, key_step, jnp.zeros((HEAD_DIM, block), F32))
            udq[slot, qat, :] = jnp.transpose(dq_t).astype(BF)
            back_dq.start(slot, qi * owners, (qi + 1) * owners)
            udk[slot, qat, :] = sums[qat, :HEAD_DIM].astype(BF)
            udv[slot, qat, :] = sums[qat, HEAD_DIM:].astype(BF)

            @pl.when((slot == 0) & (i == 0))
            def _():
                gate_a.step(1)

            @pl.when((slot == 1) & (i == 0))
            def _():
                gate_a.step(2)
                gate_b.load()
                gate_b.some(nz - 1, 0)

            @pl.when((slot == 1) & (i == 1))
            def _():
                gate_b.step(1)

            return unused_too

        lax.fori_loop(0, length // block, query_step, 0)

        @pl.when(slot == 0)
        def _():
            back_dk.start(0, 0, n)
            back_dv.start(0, 0, n)

        return unused

    def one_copy(i):
        at = aligned(i, chunk)
        return remote(two_own.at[at, :], one_in.at[at, :], tp_s.at[13 + i], tp_r.at[13 + i], place.twin)

    def through_query():
        for copy in load_wq:
            copy.wait()
        back_dq.wait()
        query.gather.start()

        def back_query(i, unused):
            at = aligned(i, chunk)
            for zy in range(n // 2):
                now = dot_nt(dq[at, :], square_block(1, zy)) * HEAD_DIM ** (-0.5)
                two_own[at, zy * blk : (zy + 1) * blk] = now.astype(BF)
            one_copy(i).start()
            return unused

        lax.fori_loop(0, 4, back_query, 0)

    def last_norm(i, gain_sum):
        one_copy(i).wait()

        def some(j, gain_sum):
            at = aligned(i * (chunk // fine) + j, fine)
            x = x_all[at, :].astype(F32)
            d1 = two_own[at, :].astype(F32) + one_in[at, :].astype(F32)
            root = lax.rsqrt(jnp.mean(x * x, axis=-1, keepdims=True) + EPSILON)
            gained = d1 * gain_one[...]
            scaled = x * root
            gain_sum = gain_sum + jnp.sum(d1 * scaled, axis=0, keepdims=True)
            slope = jnp.mean(gained * scaled, axis=-1, keepdims=True)
            mid[at, :] = mid[at, :] + root * (gained - scaled * slope)
            return gain_sum

        return lax.fori_loop(0, chunk // fine, some, gain_sum)

    give = pltpu.make_async_copy(mid.at[:, mine], r.input_grad, loc.at[19])

    def through_first_norm():
        gain_sum = lax.fori_loop(0, 4, last_norm, jnp.zeros((1, width), F32))
        for i in range(n):
            gain_part[1, i] = gain_sum[:, i * (width // n) : (i + 1) * (width // n)]
        spread_gain[1].start()
        give.start()

    def finish_all(*some):
        for line in some:
            line.finish()

    def left_all(*some):
        for line in some:
            line.left_here()

    def sent_all(*some):
        for line in some:
            line.sent()

    def err_here():
        left_err.forward()
        left_err.gone()
        left_err.finish()

    def one_here():
        left_one.gone()
        left_one.finish()

    up_a.gather.start()
    up_b.gather.start()
    left_err.start()

    with jax.named_scope("between"):
        @pl.when(jnp.logical_not(at_end))
        def _():
            for copy in ship:
                copy.wait_recv()
            for slot in range(2):
                turn_into(r.uks.at[slot], r.k_ts.at[slot])
            gate_a.step(0)
            lax.fori_loop(0, 2, one_unit, 0)
            finish_all(down_a, down_b)
            sent_all(down_a, down_b, down_c)
            up_a.load()
            up_a.some(nz - 1, 0)
            gate_b.step(2)
            finish_all(down_c)
            up_a.step(1)
            up_b.load()
            back_dk.start(1, 0, n)
            up_a.step(2)
            up_b.some(nz - 1, 0)
            back_dv.start(1, 0, n)
            through_query()
            up_b.step(1)
            err_here()
            left_all(down_a, down_b)
            finish_all(gate_a)
            left_all(down_c)
            finish_all(gate_b)
            out.load(True, gathered=True)
            up_b.step(2)
            out.some(nz - 1, 0)
            one_here()
            through_first_norm()
            out.step(1)
            query.load(True)
            left_all(gate_a)
            finish_all(up_a)
            out.step(2)
            query.some(nz - 1, 0, 1)
            left_all(gate_b)
            finish_all(up_b)
            query.step(2)
            finish_all(out, query)

    with jax.named_scope("ends"):
        @pl.when(at_end)
        def _():
            gate_b.load()
            gate_b.begin()
            finish_all(down_a, down_b, down_c)
            sent_all(down_a, down_b, down_c)
            up_a.load()
            up_a.begin()
            up_b.load()
            up_b.begin()
            left_all(down_a, down_b, down_c)
            err_here()
            out.load(True, gathered=True)
            out.begin()
            through_query()
            one_here()
            query.load(True)
            query.begin()
            through_first_norm()
            finish_all(gate_a, gate_b)
            left_all(gate_a, gate_b)
            finish_all(up_a, up_b, out, query)

    ffn_copy.wait()
    to_units.sent()
    fetch = pltpu.make_async_copy(r.mix, sums.at[: per * tokens, :], loc.at[11])
    fetch.start()
    fetch.wait()
    for i in range(per):
        at = slice(i * size, (i + 1) * size)
        attended[:, at] = (sums[i * tokens : (i + 1) * tokens, :] + r.ffn_in[:, at].astype(F32)).astype(BF)
    give_mixed = pltpu.make_async_copy(attended, r.out_mixed, loc.at[20])
    give_mixed.start()
    back_dk.wait()
    back_dv.wait()
    for g in range(2):
        spread_gain[g].wait()
        r.gains[g] = jnp.sum(gain_in[g], axis=0)

    @pl.when(at_end)
    def _():
        for copy in ship:
            copy.wait_send()

    @pl.when(jnp.logical_not(at_end))
    def _():
        for slot in range(2):
            for sent in (back_dq, back_dk, back_dv):
                sent.sent(slot)

    give.wait()
    give_mixed.wait()
    for line in lines[3:]:
        line.sent()
    for line in lines[5:]:
        line.left_here()
    for line in lines:
        line.arrived()


def results_kernel(rows, factors, *refs):
    count = len(rows)
    ins, outs, held, sems = refs[:count], refs[count : 2 * count], refs[2 * count : -1], refs[-1]
    come = [pltpu.make_async_copy(ins[i].at[: rows[i]], held[2 * i], sems.at[0, i]) for i in range(count)]
    go = [pltpu.make_async_copy(held[2 * i + 1], outs[i], sems.at[1, i]) for i in range(count)]
    for copy in come:
        copy.start()
    for i, factor in enumerate(factors):
        come[i].wait()
        if factor is not None:
            held[2 * i + 1][...] = held[2 * i][...].astype(F32) * factor
        go[i].start()
    for copy in go:
        copy.wait()


def results(*some):
    anywhere = pl.BlockSpec(memory_space=pl.ANY)
    arrays, rows, factors = zip(*some)
    shapes = [vm((k, *a.shape[1:]), a.dtype if f is None else F32) for a, k, f in some]
    held = []
    for (a, k, f), shape in zip(some, shapes):
        held += [pltpu.VMEM((k, *a.shape[1:]) if f is not None else (8, LANE), a.dtype), pltpu.VMEM(shape.shape, shape.dtype)]

    def kernel(*refs):
        count = len(rows)
        refs = list(refs)
        for i, factor in enumerate(factors):
            if factor is None:
                refs[2 * count + 2 * i] = refs[2 * count + 2 * i + 1]
        results_kernel(rows, factors, *refs)

    return pl.pallas_call(
        kernel,
        out_shape=shapes,
        in_specs=[anywhere] * len(arrays),
        out_specs=[anywhere] * len(arrays),
        scratch_shapes=[*held, pltpu.SemaphoreType.DMA((2, len(arrays)))],
        compiler_params=pltpu.CompilerParams(vmem_limit_bytes=VMEM_GRANT),
        name="results",
    )(*arrays)


def fast_device(
    n, inputs, segments, keys, values, attn_gain, query_weight, out_weight, ffn_gain, gate_weight, up_weight, down_weight,
    cotangent,
):
    rows, tok, half = inputs.shape
    tokens, width, ff = rows * tok, query_weight.shape[0], gate_weight.shape[1]
    heads, length = half // HEAD_DIM, n * tok
    geo = (n, rows, tok, width, half, heads, length)
    blk, nz, size = 2 * width // n, n // PLANE, 2 * LANE
    cols = -(-ff // size) * LANE
    firsts = (0, size, 3 * size, cols)
    thirds = [(firsts[i], firsts[i + 1] - firsts[i]) for i in range(3)]
    halves = [(0, firsts[2]), (firsts[2], cols - firsts[2])]
    cuts = tuple((kind, *cut) for kind, parts in enumerate((thirds, halves, halves)) for cut in parts)
    sizes = (ff, cols, cuts)
    square = half // 2
    n_lines = len(cuts) + 2
    dma = pltpu.SemaphoreType.DMA
    anywhere, here = pl.BlockSpec(memory_space=pl.ANY), pl.BlockSpec(memory_space=pltpu.VMEM)

    def pieces(letter, shapes):
        return {letter + str(i): shape for i, shape in shapes}

    tall, flat_left = vm((2 * cols, blk // 2), F32), vm((PLANE * tokens, width // 2), BF)
    sum_square = vm((nz + 1, blk, square), BF)
    outs = dict(
        out_mixed=vm((tokens, half), BF),
        input_grad=vm((tokens, half), F32),
        d_keys=vm((tokens, half), BF),
        d_values=vm((tokens, half), BF),
        gains=vm((2, 1, width // n), F32),
        out_down=tall,
        out_gate=tall,
        out_up=tall,
        out_out=vm((blk // 2, half), F32),
        out_query=vm((blk // 2, half), F32),
        mix=vm((half // size * tokens, size), F32),
        l_err=flat_left,
        l_one=flat_left,
        g_out=sum_square,
        g_query=sum_square,
        **pieces("m", [(i, vm((PLANE * tokens, w), BF)) for i, (kind, _, w) in enumerate(cuts) if kind > 0]),
        **pieces("g", [(i, vm((nz + 1, blk, w), BF)) for i, (_, _, w) in enumerate(cuts)]),
    )
    row = pltpu.VMEM((1, length), F32)
    act, own = pltpu.VMEM((tokens, width), BF), pltpu.VMEM((tokens, half), BF)
    split = pltpu.VMEM((2, tokens, width // 2), BF)
    hid = pltpu.VMEM((tokens, 2 * cols), BF)
    gain = pltpu.VMEM((2, n, 1, width // n), F32)
    left = pltpu.VMEM((PLANE * tokens, width // 2), BF)
    two = pltpu.VMEM((2, length, HEAD_DIM), BF)
    move, move_square = (pltpu.VMEM((nz - 1, blk, c), BF) for c in (cols, square))
    total, total_square = (pltpu.VMEM((blk, c), F32) for c in (cols, square))
    taken = pltpu.VMEM((PLANE * tokens, square), BF)
    scratch = dict(
        mid=pltpu.VMEM((tokens, width), F32),
        x_all=act, cot_all=act, two_norm=act, two_own=act, two_in=act, one_in=act, mixed=split, err=split, one=split,
        wbuf=pltpu.VMEM((8, size, width), BF),
        attended=own, dq=own, ffn_in=own, hidden=hid, d_gate=hid, d_up=hid,
        sums=pltpu.VMEM((length, size), F32),
        uqs=two, uks=two, uvs=two, uos=two, udo=two, udq=two, udk=two, udv=two,
        delta=row, seg_row=row, lses=pltpu.VMEM((2, 1, length), F32),
        seg_all=pltpu.VMEM((n, 1, tok), segments.dtype),
        seg_col=pltpu.VMEM((length, LANE), F32),
        k_ts=pltpu.VMEM((2, HEAD_DIM, length), BF),
        gain_part=gain, gain_in=gain,
        s_first=move, s_second=move, s_out=move_square, s_query=move_square,
        t_first=total, t_second=total, t_out=total_square, t_query=total_square,
        turned=pltpu.VMEM((cols, blk), F32),
        mv=pltpu.VMEM((PLANE * tokens, cols), BF), mv_out=taken, mv_query=taken,
        lv_one=left, lv_two=left,
        acc=total,
        stage=pltpu.VMEM((blk, cols), BF),
        tp_s=dma((17,)), tp_r=dma((17,)), a_s=dma((7,)), a_r=dma((7,)),
        me_s=dma((n_lines, 3)), me_r=dma((n_lines, 3)), le_s=dma((4, 3)), le_r=dma((4, 3)),
        c_s=dma((n_lines, nz - 1)), c_r=dma((n_lines, nz + 1)),
        e_s=dma((n_lines,)), e_r=dma((n_lines,)), e_l=dma((n_lines,)),
        sh_s=dma((5,)), sh_r=dma((5,)), u_s=dma((1,)), u_r=dma((2,)), u_l=dma((2,)),
        f_s=dma((3, 2)), f_r=dma((3,)), f_l=dma((3, 2)),
        loc=dma((21,)), g_loc=dma((n_lines,)), l_loc=dma((4,)), work_sem=dma((3,)),
        w_sem=dma((4, 2, 2)), tail_sem=dma((4, 2, 2)), o_sem=dma((4, n // 2)),
    )
    names = (*outs, *scratch)

    def flat(a):
        return a.reshape(tokens, half)

    segs = segments.reshape(rows, 1, tok)
    got = pl.pallas_call(
        functools.partial(layer_kernel, geo, sizes, names),
        out_shape=list(outs.values()),
        in_specs=[anywhere] * 10 + [here] * 2,
        out_specs=[here if i == 4 else anywhere for i in range(len(outs))],
        scratch_shapes=list(scratch.values()),
        compiler_params=pltpu.CompilerParams(
            collective_id=0, has_side_effects=True, vmem_limit_bytes=VMEM_GRANT
        ),
        name="layer",
    )(
        flat(inputs), flat(cotangent), flat(keys), flat(values), segs, gate_weight.T, up_weight.T, down_weight.T,
        out_weight, query_weight, attn_gain.reshape(1, width), ffn_gain.reshape(1, width),
    )
    got = types.SimpleNamespace(**dict(zip(outs, got)))

    def shaped(a):
        return a.reshape(rows, tok, half)

    d_keys, d_values, g_query, g_down, g_gate, g_up, input_grad, mixed, g_out = results(
        (got.d_keys, tokens, 1.0),
        (got.d_values, tokens, 1.0),
        (got.out_query, blk // 2, HEAD_DIM ** (-0.5)),
        (got.out_down, ff, None),
        (got.out_gate, ff, None),
        (got.out_up, ff, None),
        (got.input_grad, tokens, None),
        (got.out_mixed, tokens, None),
        (got.out_out, blk // 2, None),
    )
    return (
        shaped(mixed),
        shaped(input_grad),
        shaped(d_keys),
        shaped(d_values),
        got.gains[1, 0],
        g_query,
        g_out,
        got.gains[0, 0],
        g_gate.T,
        g_up.T,
        g_down.T,
    )


def inverse_root(stream):
    return lax.rsqrt(jnp.mean(stream * stream, axis=-1, keepdims=True) + EPSILON)


def key_mask(doc_start, query_pos, begin, row_count):
    key_pos = begin + jnp.arange(row_count, dtype=jnp.int32)
    earlier = key_pos[None, None, :] <= query_pos[None, :, None]
    same_doc = key_pos[None, None, :] >= doc_start[:, :, None]
    return (earlier & same_doc)[:, None]


def per_device(
    inputs,
    segments,
    keys,
    values,
    attn_gain,
    query_weight,
    out_weight,
    ffn_gain,
    gate_weight,
    up_weight,
    down_weight,
    cotangent,
):
    batch_rows, local_tokens, half_width = inputs.shape
    local_heads = half_width // HEAD_DIM
    seq_devices = lax.axis_size("seq")
    row_length = local_tokens * seq_devices
    seq_index = lax.axis_index("seq")
    tp_index = lax.axis_index("tp")
    query_scale = HEAD_DIM ** (-0.5)
    bfloat = jnp.bfloat16
    single = jnp.float32
    whole = lax.all_gather(inputs, "tp", axis=2, tiled=True).astype(single)
    root_one = inverse_root(whole)
    scaled_one = whole * root_one
    normed_one = (scaled_one * attn_gain).astype(bfloat)
    query = (
        jnp.einsum("rtd,de->rte", normed_one, query_weight, preferred_element_type=single)
        * query_scale
    ).astype(bfloat)
    query_heads = query.reshape(batch_rows, local_tokens, local_heads, HEAD_DIM)
    bins = jnp.arange(CUTS + 1, dtype=jnp.int32)
    onehot = (segments[:, :, None] == bins[None, None, :]).astype(single)
    totals = lax.psum(jnp.sum(onehot, axis=1), "seq")
    ends = jnp.cumsum(totals, axis=-1)
    before = ends - totals
    doc_start = jnp.sum(onehot * before[:, None, :], axis=-1).astype(jnp.int32)
    query_pos = seq_index * local_tokens + jnp.arange(local_tokens, dtype=jnp.int32)
    first_needed = jnp.min(doc_start)
    last_needed = seq_index * local_tokens + local_tokens - 1
    start_state = (
        jnp.full((batch_rows, local_heads, local_tokens), NEGATIVE_FILL, single),
        jnp.zeros((batch_rows, local_heads, local_tokens), single),
        jnp.zeros((batch_rows, local_heads, local_tokens, HEAD_DIM), single),
    )
    key_piece = lax.all_gather(keys, "seq", axis=1, tiled=True)
    value_piece = lax.all_gather(values, "seq", axis=1, tiled=True)
    piece_rows = key_piece.shape[1]
    fold_key_block = math.gcd(piece_rows, 512)

    def fold_step(block_index, state):
        running_max, running_sum, running_out = state
        begin = block_index * fold_key_block

        def fold_work(unused):
            key_heads = lax.dynamic_slice_in_dim(
                key_piece, block_index * fold_key_block, fold_key_block, 1
            ).reshape(batch_rows, fold_key_block, local_heads, HEAD_DIM)
            value_heads = lax.dynamic_slice_in_dim(
                value_piece, block_index * fold_key_block, fold_key_block, 1
            ).reshape(batch_rows, fold_key_block, local_heads, HEAD_DIM)
            scores = jnp.einsum(
                "rqhe,rkhe->rhqk", query_heads, key_heads, preferred_element_type=single
            )
            allowed = key_mask(doc_start, query_pos, begin, fold_key_block)
            scores = jnp.where(allowed, scores, NEGATIVE_FILL)
            new_max = jnp.maximum(running_max, jnp.max(scores, axis=-1))
            weights = jnp.where(allowed, jnp.exp(scores - new_max[..., None]), 0.0)
            decay = jnp.exp(running_max - new_max)
            new_sum = running_sum * decay + jnp.sum(weights, axis=-1)
            new_out = running_out * decay[..., None] + jnp.einsum(
                "rhqk,rkhe->rhqe",
                weights.astype(bfloat),
                value_heads,
                preferred_element_type=single,
            )
            return (new_max, new_sum, new_out)

        def keep_state(unused):
            return (running_max, running_sum, running_out)

        needed = (begin <= last_needed) & (begin + fold_key_block - 1 >= first_needed)
        return lax.cond(needed, fold_work, keep_state, 0)

    running_max, running_sum, running_out = lax.fori_loop(
        0, piece_rows // fold_key_block, fold_step, start_state
    )
    log_total = running_max + jnp.log(running_sum)
    attended = running_out / running_sum[..., None]
    attended_low = (
        attended.transpose(0, 2, 1, 3).reshape(batch_rows, local_tokens, half_width).astype(bfloat)
    )
    branch = jnp.einsum("rth,dh->rtd", attended_low, out_weight, preferred_element_type=single)
    middle = whole + lax.psum(branch.astype(jnp.bfloat16), "tp").astype(jnp.float32)
    middle_share = lax.dynamic_slice_in_dim(middle, tp_index * half_width, half_width, 2)
    root_two = inverse_root(middle)
    scaled_two = middle * root_two
    normed_two = (scaled_two * ffn_gain).astype(bfloat)
    gate = jnp.einsum("rtd,df->rtf", normed_two, gate_weight, preferred_element_type=single)
    up_proj = jnp.einsum("rtd,df->rtf", normed_two, up_weight, preferred_element_type=single)
    sigma = jax.nn.sigmoid(gate)
    activated = gate * sigma
    hidden = (activated * up_proj).astype(bfloat)
    ffn_part = jnp.einsum("rtf,df->rtd", hidden, down_weight, preferred_element_type=single)
    output = (
        middle_share
        + lax.psum_scatter(
            ffn_part.astype(jnp.bfloat16), "tp", scatter_dimension=2, tiled=True
        ).astype(jnp.float32)
    ).astype(bfloat)
    grad_out = lax.all_gather(cotangent, "tp", axis=2, tiled=True)
    d_hidden = jnp.einsum("rtd,df->rtf", grad_out, down_weight, preferred_element_type=single)
    d_gate = (d_hidden * up_proj * sigma * (1.0 + gate * (1.0 - sigma))).astype(bfloat)
    d_up = (d_hidden * activated).astype(bfloat)
    d_two_part = jnp.einsum(
        "rtf,df->rtd", d_gate, gate_weight, preferred_element_type=single
    ) + jnp.einsum("rtf,df->rtd", d_up, up_weight, preferred_element_type=single)
    d_two = lax.psum(d_two_part.astype(jnp.bfloat16), "tp").astype(jnp.float32)
    gained_two = d_two * ffn_gain
    d_middle = (
        grad_out.astype(single)
        + root_two * gained_two
        - middle * root_two**3 * jnp.mean(gained_two * middle, axis=-1, keepdims=True)
    )
    normed_rows = normed_two
    gate_term = jnp.einsum("rtd,rtf->df", normed_rows, d_gate, preferred_element_type=single)
    up_term = jnp.einsum("rtd,rtf->df", normed_rows, d_up, preferred_element_type=single)
    down_term = jnp.einsum("rtd,rtf->df", grad_out, hidden, preferred_element_type=single)
    gain_term = jnp.sum(d_two * scaled_two, axis=(0, 1))
    gate_grad, up_grad, down_grad, ffn_gain_grad = lax.psum_scatter(
        (gate_term, up_term, down_term, gain_term), "seq", scatter_dimension=0, tiled=True
    )
    error = d_middle.astype(bfloat)
    d_attended = jnp.einsum("rtd,dh->rth", error, out_weight, preferred_element_type=single).astype(
        bfloat
    )
    d_heads = d_attended.reshape(batch_rows, local_tokens, local_heads, HEAD_DIM)
    carried = jnp.einsum("rqhe,rhqe->rhq", d_heads.astype(single), attended)
    key_all, value_all = (
        lax.all_gather(keys, "seq", axis=1, tiled=True),
        lax.all_gather(values, "seq", axis=1, tiled=True),
    )
    key_block = math.gcd(row_length, 512)

    def block_terms(begin):
        key_heads = lax.dynamic_slice_in_dim(key_all, begin, key_block, 1).reshape(
            batch_rows, key_block, local_heads, HEAD_DIM
        )
        value_heads = lax.dynamic_slice_in_dim(value_all, begin, key_block, 1).reshape(
            batch_rows, key_block, local_heads, HEAD_DIM
        )
        scores = jnp.einsum(
            "rqhe,rkhe->rhqk", query_heads, key_heads, preferred_element_type=single
        )
        allowed = key_mask(doc_start, query_pos, begin, key_block)
        probs = jnp.where(
            allowed, jnp.exp(jnp.where(allowed, scores, NEGATIVE_FILL) - log_total[..., None]), 0.0
        )
        d_probs = jnp.einsum("rqhe,rkhe->rhqk", d_heads, value_heads, preferred_element_type=single)
        d_scores = (probs * (d_probs - carried[..., None])).astype(bfloat)
        query_part = jnp.einsum(
            "rhqk,rkhe->rhqe", d_scores, key_heads, preferred_element_type=single
        )
        return (probs, d_scores, query_part)

    query_zero = jnp.zeros((batch_rows, local_heads, local_tokens, HEAD_DIM), single)

    def back_step(block_index, state):
        d_query, key_terms, value_terms = state
        begin = block_index * key_block

        def back_work(unused):
            probs, d_scores, query_part = block_terms(begin)
            value_part = jnp.einsum(
                "rhqk,rqhe->rkhe", probs.astype(bfloat), d_heads, preferred_element_type=single
            )
            key_part = jnp.einsum(
                "rhqk,rqhe->rkhe", d_scores, query_heads, preferred_element_type=single
            )
            return (
                query_part,
                key_part.reshape(batch_rows, key_block, half_width),
                value_part.reshape(batch_rows, key_block, half_width),
            )

        def skip_block(unused):
            empty_rows = jnp.zeros((batch_rows, key_block, half_width), single)
            return (jnp.zeros_like(d_query), empty_rows, empty_rows)

        needed = (begin <= last_needed) & (begin + key_block - 1 >= first_needed)
        query_part, key_part, value_part = lax.cond(needed, back_work, skip_block, 0)
        return (
            d_query + query_part,
            lax.dynamic_update_slice_in_dim(key_terms, key_part, begin, 1),
            lax.dynamic_update_slice_in_dim(value_terms, value_part, begin, 1),
        )

    back_start = (
        query_zero,
        jnp.zeros((batch_rows, row_length, half_width), single),
        jnp.zeros((batch_rows, row_length, half_width), single),
    )
    d_query, key_terms, value_terms = lax.fori_loop(
        0, row_length // key_block, back_step, back_start
    )
    key_grad, value_grad = (
        lax.psum_scatter(key_terms, "seq", scatter_dimension=1, tiled=True),
        lax.psum_scatter(value_terms, "seq", scatter_dimension=1, tiled=True),
    )
    d_query_rows = (
        d_query.transpose(0, 2, 1, 3).reshape(batch_rows, local_tokens, half_width).astype(bfloat)
    )
    d_one_part = (
        jnp.einsum("rte,de->rtd", d_query_rows, query_weight, preferred_element_type=single)
        * query_scale
    )
    d_one = lax.psum(d_one_part.astype(jnp.bfloat16), "tp").astype(jnp.float32)
    gained_one = d_one * attn_gain
    d_whole = (
        d_middle
        + root_one * gained_one
        - whole * root_one**3 * jnp.mean(gained_one * whole, axis=-1, keepdims=True)
    )
    input_grad = lax.dynamic_slice_in_dim(d_whole, tp_index * half_width, half_width, 2)
    normed_rows = normed_one
    query_term = (
        jnp.einsum("rtd,rte->de", normed_rows, d_query_rows, preferred_element_type=single)
        * query_scale
    )
    out_term = jnp.einsum("rtd,rth->dh", error, attended_low, preferred_element_type=single)
    gain_term = jnp.sum(d_one * scaled_one, axis=(0, 1))
    query_grad, out_grad, attn_gain_grad = lax.psum_scatter(
        (query_term, out_term, gain_term), "seq", scatter_dimension=0, tiled=True
    )
    return (
        output,
        input_grad,
        key_grad,
        value_grad,
        attn_gain_grad,
        query_grad,
        out_grad,
        ffn_gain_grad,
        gate_grad,
        up_grad,
        down_grad,
    )


def solution(mesh):
    in_specs = (
        P(None, "seq", "tp"),
        P(None, "seq"),
        P(None, "seq", "tp"),
        P(None, "seq", "tp"),
        P(),
        P(None, "tp"),
        P(None, "tp"),
        P(),
        P(None, "tp"),
        P(None, "tp"),
        P(None, "tp"),
        P(None, "seq", "tp"),
    )
    out_specs = (
        P(None, "seq", "tp"),
        P(None, "seq", "tp"),
        P(None, "seq", "tp"),
        P(None, "seq", "tp"),
        P("seq"),
        P("seq", "tp"),
        P("seq", "tp"),
        P("seq"),
        P("seq", "tp"),
        P("seq", "tp"),
        P("seq", "tp"),
    )
    n = mesh.shape["seq"]

    def step(inputs, *others):
        rows, tok, half = inputs.shape
        units = rows * (half // HEAD_DIM)
        if units == n == PLANE * PLANE and tok == LANE and mesh.shape["tp"] == 2 and -(-others[7].shape[1] // (2 * LANE)) % 2:
            return fast_device(n, inputs, *others)
        return per_device(inputs, *others)

    return jax.shard_map(
        step, mesh=mesh, in_specs=in_specs, out_specs=out_specs, check_vma=False
    )
```

profile of v0, /device:TPU:0, one launch (start us, length us, event | category | flops | bytes accessed | tf_op | source)
XLA Modules:
  0.0 307.5 jit_solution(5994303516566745604)
XLA Ops:
  0.6 299.1 %layer.1 = (bf16[256,1024]{1,0:T(8,128)(2,1)}, f32[256,1024]{1,0:T(8,128)}, bf16[256,1024]{1,0:T(8,128)(2,1)}, bf16[256,1024]{1,0:T(8,128)(2,1)}, f32[2,1,128]{2...) custom-call(bf16[256,1024]{1,0:T(8,128)(2,1)} %bitcast.24, ...), custom_call_target="tpu_custom_call" | custom-call | tf_op jit(solution)/shard_map/layer/pallas_call | solution.py:1313
  299.7 1.2 slice_bitcast_fusion
  300.9 6.4 %results.1 = (f32[256,1024]{1,0:T(8,128)}, f32[256,1024]{1,0:T(8,128)}, f32[128,1024]{1,0:T(8,128)}, f32[2752,128]{1,0:T(8,128)}, f32[2752,128]{1,0:T(8,128)}, /...) custom-call(bf16[256,1024]{1,0:T(8,128)(2,1)} %get-tuple-element.30.refs_0_, ...), custom_call_target="tpu_custom_call" | custom-call | tf_op jit(solution)/shard_map/results/pallas_call | solution.py:1214
where the time goes:
time: 310 us; the launch traced here: 307 us
  Pallas kernels  305 us (98%)
    pallas_call x1, Pallas kernels, fast_device(): pl.pallas_call(functools.partial(layer_kernel, geo, sizes, names), out_sh...  299 us
    pallas_call x1, Pallas kernels, results(): pl.pallas_call(kernel, out_shape=shapes, in_specs=[anywhere] * len(arrays...  6.4 us

commit v1 on v0

--- a/solution.py
+++ b/solution.py
@@ -188,10 +188,12 @@
         c = place.c
         self.own = pltpu.make_async_copy(half(c), to, local)
         self.away = [
-            remote(half(c), to, send.at[0], recv.at[0], place.side),
-            remote(half(1 - c), to, send.at[1], recv.at[1], place.cross),
-            remote(half(1 - c), to, send.at[2], recv.at[2], place.core),
+            remote(half(c), to, send, recv, place.side),
+            remote(half(1 - c), to, send, recv, place.cross),
+            remote(half(1 - c), to, send, recv, place.core),
         ]
+        bulk = land.at[: (PLANE - 1) * tokens, :]
+        self.all = remote(bulk, bulk, send, recv, place.core)
 
     def start(self):
         self.own.start()
@@ -200,8 +202,7 @@
 
     def wait(self):
         self.own.wait()
-        for copy in self.away:
-            copy.wait()
+        self.all.wait()
 
 
 class Line:
@@ -1156,7 +1157,7 @@
     back_dv.wait()
     for g in range(2):
         spread_gain[g].wait()
-        r.gains[g] = jnp.sum(gain_in[g], axis=0)
+        (r.gain_two, r.gain_one)[g][...] = jnp.sum(gain_in[g], axis=0)
 
     @pl.when(at_end)
     def _():
@@ -1252,7 +1253,8 @@
         input_grad=vm((tokens, half), F32),
         d_keys=vm((tokens, half), BF),
         d_values=vm((tokens, half), BF),
-        gains=vm((2, 1, width // n), F32),
+        gain_one=vm((1, width // n), F32),
+        gain_two=vm((1, width // n), F32),
         out_down=tall,
         out_gate=tall,
         out_up=tall,
@@ -1296,7 +1298,7 @@
         acc=total,
         stage=pltpu.VMEM((blk, cols), BF),
         tp_s=dma((17,)), tp_r=dma((17,)), a_s=dma((7,)), a_r=dma((7,)),
-        me_s=dma((n_lines, 3)), me_r=dma((n_lines, 3)), le_s=dma((4, 3)), le_r=dma((4, 3)),
+        me_s=dma((n_lines,)), me_r=dma((n_lines,)), le_s=dma((4, 3)), le_r=dma((4, 3)),
         c_s=dma((n_lines, nz - 1)), c_r=dma((n_lines, nz + 1)),
         e_s=dma((n_lines,)), e_r=dma((n_lines,)), e_l=dma((n_lines,)),
         sh_s=dma((5,)), sh_r=dma((5,)), u_s=dma((1,)), u_r=dma((2,)), u_l=dma((2,)),
@@ -1314,7 +1316,7 @@
         functools.partial(layer_kernel, geo, sizes, names),
         out_shape=list(outs.values()),
         in_specs=[anywhere] * 10 + [here] * 2,
-        out_specs=[here if i == 4 else anywhere for i in range(len(outs))],
+        out_specs=[here if i in (4, 5) else anywhere for i in range(len(outs))],
         scratch_shapes=list(scratch.values()),
         compiler_params=pltpu.CompilerParams(
             collective_id=0, has_side_effects=True, vmem_limit_bytes=VMEM_GRANT
@@ -1329,7 +1331,7 @@
     def shaped(a):
         return a.reshape(rows, tok, half)
 
-    d_keys, d_values, g_query, g_down, g_gate, g_up, input_grad, mixed, g_out = results(
+    d_keys, d_values, g_query, g_down, g_gate, g_up, input_grad, mixed, g_out, grad_one, grad_two = results(
         (got.d_keys, tokens, 1.0),
         (got.d_values, tokens, 1.0),
         (got.out_query, blk // 2, HEAD_DIM ** (-0.5)),
@@ -1339,16 +1341,18 @@
         (got.input_grad, tokens, None),
         (got.out_mixed, tokens, None),
         (got.out_out, blk // 2, None),
+        (got.gain_one, 1, None),
+        (got.gain_two, 1, None),
     )
     return (
         shaped(mixed),
         shaped(input_grad),
         shaped(d_keys),
         shaped(d_values),
-        got.gains[1, 0],
+        grad_one.reshape(width // n),
         g_query,
         g_out,
-        got.gains[0, 0],
+        grad_two.reshape(width // n),
         g_gate.T,
         g_up.T,
         g_down.T,

time: 310 us -> 308 us (level)
  no operation moved by 1% of the time
where the time goes in v1:
time: 308 us; the launch traced here: 306 us
  Pallas kernels  305 us (99%)
    pallas_call x1, Pallas kernels, fast_device(): pl.pallas_call(functools.partial(layer_kernel, geo, sizes, names), out_sh...  299 us
    pallas_call x1, Pallas kernels, results(): pl.pallas_call(kernel, out_shape=shapes, in_specs=[anywhere] * len(arrays...  6.45 us

profile of v1, /device:TPU:0, one launch (start us, length us, event | category | flops | bytes accessed | tf_op | source)
XLA Modules:
  0.0 306.0 jit_solution(7891024740178783436)
XLA Ops:
  0.6 298.7 %layer.1 = (bf16[256,1024]{1,0:T(8,128)(2,1)}, f32[256,1024]{1,0:T(8,128)}, bf16[256,1024]{1,0:T(8,128)(2,1)}, bf16[256,1024]{1,0:T(8,128)(2,1)}, f32[1,128]{1,0...) custom-call(bf16[256,1024]{1,0:T(8,128)(2,1)} %bitcast.22, ...), custom_call_target="tpu_custom_call" | custom-call | tf_op jit(solution)/shard_map/layer/pallas_call | solution.py:1315
  299.4 6.4 %results.1 = (f32[256,1024]{1,0:T(8,128)}, f32[256,1024]{1,0:T(8,128)}, f32[128,1024]{1,0:T(8,128)}, f32[2752,128]{1,0:T(8,128)}, f32[2752,128]{1,0:T(8,128)}, /...) custom-call(bf16[256,1024]{1,0:T(8,128)(2,1)} %get-tuple-element.33., ...), custom_call_target="tpu_custom_call" | custom-call | tf_op jit(solution)/shard_map/results/pallas_call | solution.py:1215
